TPU v7x, 32 devices: a whole 2x2x4 slice. The times are simulated.
32 devices in a mesh: col: 4 (over y, x), tok: 8 (over z, core).
Axes of the slice: x: 2, y: 2, z: 4, core: 2. Of those that a mesh axis runs over, the one named last changes fastest.
Arguments:
- activations: bfloat16 [8192, 8192], P('tok', 'col'), may hold values from -6 to 6
Outputs:
- factor: float32 [8192, 8192], P(('col', 'tok'))
All inputs are finite; a program needn't handle non-finite values.
Results may differ from a plain program's by a relative error of at most 0.0003.
Values may be sent and summed in bfloat16 or wider, within the bound.
No kernel may reach another device: no remote copies, remote signals or barrier semaphores. Data moves between devices by JAX's collectives and lax.ppermute only.
A program may use at most 128 MiB of HBM per device.

v0:
```python
import jax
import jax.numpy as jnp
from jax import lax
from jax.sharding import PartitionSpec as P

contract_first = (((0,), (0,)), ((), ()))


def passed_along(value, axis, by):
    size = lax.axis_size(axis)
    return lax.ppermute(value, axis, [(i, (i + by) % size) for i in range(size)])


def make_term(left_block, right_block):
    return lax.dot_general(
        left_block, right_block, contract_first, preferred_element_type=jnp.float32
    )


def shards(activations):
    block_width = activations.shape[1]
    token_ranks = lax.axis_size("tok")
    column_ranks = lax.axis_size("col")
    share_rows = block_width // token_ranks
    total_tokens = activations.shape[0] * token_ranks
    half_loop = column_ranks // 2
    fetched = [activations]
    for offset in range(1, half_loop + 1):
        fetched.append(passed_along(fetched[-1], "col", -1))
    tile_pairs = []
    for offset in range(half_loop + 1):
        tile_pairs.append((fetched[0], fetched[offset]))
    summed = [
        lax.psum_scatter(make_term(left_block, right_block), "tok", scatter_dimension=0, tiled=True)
        for left_block, right_block in tile_pairs
    ]
    pieces = [None] * column_ranks
    pieces[0] = summed[0]
    pieces[half_loop] = summed[half_loop]
    for offset in range(1, half_loop):
        reduced_tile = summed[offset]
        turned = lax.all_to_all(reduced_tile, "tok", split_axis=1, concat_axis=0, tiled=True).T
        own_piece, sent_piece = (reduced_tile, turned)
        pieces[offset] = own_piece
        pieces[column_ranks - offset] = passed_along(sent_piece, "col", offset)
    stacked = jnp.stack(pieces)
    ordered = jnp.roll(stacked, lax.axis_index("col"), axis=0)
    token_sums = jnp.transpose(ordered, (1, 0, 2)).reshape(share_rows, column_ranks * block_width)
    return token_sums / jnp.float32(total_tokens)


def solution(mesh):
    in_specs = (P("tok", "col"),)
    out_specs = P(("col", "tok"), None)
    return jax.shard_map(shards, mesh=mesh, in_specs=in_specs, out_specs=out_specs, check_vma=False)
```

profile of v0, /device:TPU:0, one launch (start us, length us, event | category | flops | bytes accessed | tf_op | source)
XLA Modules:
  0.0 715.8 jit_solution(16235113252800301447)
XLA Ops:
  6.5 3.9 collective-permute-start
  10.4 90.1 %collective-permute-done = bf16[1024,2048]{1,0:T(8,128)(2,1)S(1)} collective-permute-done((bf16[1024,2048]{1,0:T(8,128)(2,1)}, bf16[1024,2048]{1,0:T(8,128)(2,1)S(1)}, u32[]{:S(2)}, u32[]{:S(2)}) %collective-permute-start) | collective-permute-done | bytes 4194336 | tf_op jit(solution)/shard_map/ppermute | solution.py:11
  100.6 2.0 copy-done.3
  102.6 14.1 %fusion.1 = f32[2048,2048]{1,0:T(8,128)} fusion(bf16[1024,2048]{1,0:T(8,128)(2,1)} %param.1, bf16[1024,2048]{1,0:T(8,128)(2,1)S(1)} %collective-permute-done), kind=kOutput, calls=%fused_computation.10 | convolution fusion | flops 8589934592 | bytes 25165824 | tf_op jit(solution)/shard_map/dot_general | solution.py:15
  116.7 15.2 %fusion = f32[2048,2048]{1,0:T(8,128)} fusion(bf16[1024,2048]{1,0:T(8,128)(2,1)} %param.1), kind=kOutput, calls=%fused_computation.9 | convolution fusion | flops 8589934592 | bytes 20971520 | tf_op jit(solution)/shard_map/dot_general | solution.py:15
  132.0 3.5 collective-permute-start.1
  135.5 89.3 %collective-permute-done.1 = bf16[1024,2048]{1,0:T(8,128)(2,1)S(1)} collective-permute-done((bf16[1024,2048]{1,0:T(8,128)(2,1)}, bf16[1024,2048]{1,0:T(8,128)(2,1)S(1)}, u32[]{:S(2)}, u32[]{:S(2)}) %collective-permute-start.1) | collective-permute-done | bytes 4194336 | tf_op jit(solution)/shard_map/ppermute | solution.py:11
  224.8 14.1 %fusion.2 = f32[2048,2048]{1,0:T(8,128)} fusion(bf16[1024,2048]{1,0:T(8,128)(2,1)} %param.1, bf16[1024,2048]{1,0:T(8,128)(2,1)S(1)} %collective-permute-done.1), kind=kOutput, calls=%fused_computation.11 | convolution fusion | flops 8589934592 | bytes 25165824 | tf_op jit(solution)/shard_map/dot_general | solution.py:15
  239.0 48.2 %reduce-scatter.6.cloned.1.call-done = f32[256,2048]{1,0:T(8,128)} async-done(((f32[2048,2048]{1,0:T(8,128)}), f32[256,2048]{1,0:T(8,128)}) %reduce-scatter.6.cloned.1.call-update) | async-done | bytes 2097168 | tf_op jit(solution)/shard_map/reduce_scatter | solution.py:34
  287.2 3.0 copy.10
  290.2 86.4 %all_to_all.19 = f32[256,8,256]{0,2,1:T(8,128)S(1)} all-to-all(f32[256,8,256]{0,2,1:T(8,128)} %bitcast.29), channel_id=1, replica_groups=mesh['col'=4,'tok'=8] {'tok'}, dimensions={1} | all-to-all | bytes 4194304 | tf_op jit(solution)/shard_map/all_to_all | solution.py:42
  376.6 1.6 copy.11
  378.2 1.5 collective-permute-start.2
  379.6 109.4 %reduce-scatter.4.cloned.1.call-done = f32[256,2048]{1,0:T(8,128)} async-done(((f32[2048,2048]{1,0:T(8,128)}), f32[256,2048]{1,0:T(8,128)}) %reduce-scatter.4.cloned.1.call-update) | async-done | bytes 2097168 | tf_op jit(solution)/shard_map/reduce_scatter | solution.py:34
  489.1 3.2 bitcast_dynamic-update-slice_fusion.6
  493.7 175.5 %reduce-scatter.8.cloned.1.call-done = f32[256,2048]{1,0:T(8,128)} async-done(((f32[2048,2048]{1,0:T(8,128)}), f32[256,2048]{1,0:T(8,128)}) %reduce-scatter.8.cloned.1.call-update) | async-done | bytes 2097168 | tf_op jit(solution)/shard_map/reduce_scatter | solution.py:34
  669.2 3.3 bitcast_dynamic-update-slice_fusion.2
  672.5 3.2 bitcast_dynamic-update-slice_fusion
  675.6 1.5 bitcast_dynamic-update-slice_fusion.7
  677.1 1.5 bitcast_dynamic-update-slice_fusion.5
  680.1 3.1 bitcast_dynamic-update-slice_fusion.1
  683.2 8.4 %multiply_bitcast_fusion = f32[256,4,2048]{2,0,1:T(8,128)} fusion(f32[8,256,2048]{2,1,0:T(8,128)} %bitcast_dynamic-update-slice_fusion.1, s32[]{:T(128)S(6)} %select_n.14), kind=kLoop, calls=%fused_computation | loop fusion | flops 2097152 | bytes 16777220 | tf_op jit(solution)/shard_map/div | solution.py:49
  691.6 8.7 %copy.8 = f32[256,4,2048]{0,2,1:T(8,128)} copy(f32[256,4,2048]{2,0,1:T(8,128)} %multiply_bitcast_fusion) | data formatting | bytes 16777216 | tf_op jit(solution)/shard_map/div | solution.py:49
  700.3 8.9 %copy.9 = f32[256,8192]{1,0:T(8,128)} copy(f32[256,8192]{0,1:T(8,128)} %bitcast.27) | data formatting | bytes 16777216 | tf_op jit(solution)/shard_map/div | solution.py:49
  (16 shorter events, 3.1 us)
Async XLA Ops:
  6.5 280.6 %reduce-scatter.6.cloned.1.call-start = ((), (), s32[]{:S(2)}) async-start(), calls=%async_computation.5 | async-start | bytes 18874368 | tf_op jit(solution)/shard_map/reduce_scatter | solution.py:34
  6.5 94.0 %collective-permute-start = (bf16[1024,2048]{1,0:T(8,128)(2,1)}, bf16[1024,2048]{1,0:T(8,128)(2,1)S(1)}, u32[]{:S(2)}, u32[]{:S(2)}) collective-permute-start(bf16[1024,2048]{1,0:T(8,128)(2,1)} %param.1), channel_id=1, source_target_pairs={{0,24},{8,0},{16,8},{24,16},{1,25},{9,1},{17,9},{25,17},{2,26},{10... | collective-permute-start | bytes 12582920 | tf_op jit(solution)/shard_map/ppermute | solution.py:11
  100.6 2.0 copy-start.3
  116.7 372.4 %reduce-scatter.4.cloned.1.call-start = ((), (), s32[]{:S(2)}) async-start(), calls=%async_computation.4 | async-start | bytes 18874368 | tf_op jit(solution)/shard_map/reduce_scatter | solution.py:34
  132.0 537.2 %reduce-scatter.8.cloned.1.call-start = ((), (), s32[]{:S(2)}) async-start(), calls=%async_computation.6 | async-start | bytes 18874368 | tf_op jit(solution)/shard_map/reduce_scatter | solution.py:34
  132.0 92.8 %collective-permute-start.1 = (bf16[1024,2048]{1,0:T(8,128)(2,1)}, bf16[1024,2048]{1,0:T(8,128)(2,1)S(1)}, u32[]{:S(2)}, u32[]{:S(2)}) collective-permute-start(bf16[1024,2048]{1,0:T(8,128)(2,1)} %copy-done.3), channel_id=1, source_target_pairs={{0,24},{8,0},{16,8},{24,16},{1,25},{9,1},{17,9},{25,17},{2,26},{10... | collective-permute-start | bytes 12582920 | tf_op jit(solution)/shard_map/ppermute | solution.py:11
  287.1 205.1 %copy-start = (f32[256,2048]{1,0:T(8,128)S(1)}, f32[256,2048]{1,0:T(8,128)}, u32[]{:S(2)}) copy-start(f32[256,2048]{1,0:T(8,128)} %reduce-scatter.6.cloned.1.call-done) | copy-start | bytes 6291460
  378.2 294.3 %collective-permute-start.2 = (f32[256,2048]{1,0:T(8,128)}, f32[256,2048]{1,0:T(8,128)}, u32[]{:S(2)}, u32[]{:S(2)}) collective-permute-start(f32[256,2048]{1,0:T(8,128)} %bitcast.5), channel_id=1, source_target_pairs={{0,8},{8,16},{16,24},{24,0},{1,9},{9,17},{17,25},{25,1},{2,10},{10... | collective-permute-start | bytes 6291464 | tf_op jit(solution)/shard_map/ppermute | solution.py:11
  669.2 6.5 copy-start.1
  669.2 9.4 %copy-start.2 = (f32[256,2048]{1,0:T(8,128)S(1)}, f32[256,2048]{1,0:T(8,128)}, u32[]{:S(2)}) copy-start(f32[256,2048]{1,0:T(8,128)} %reduce-scatter.8.cloned.1.call-done) | copy-start | bytes 6291460
Sparse Core Ops, SparseCore 0:
  116.8 170.3 reduce-scatter.5
  289.5 199.5 reduce-scatter.3
  491.4 177.6 reduce-scatter.7
where the time goes:
time: 716 us
  waiting for transfers between devices  513 us (72%)
  blocking collectives  86.4 us (12%)
  matrix products  43.4 us (6%)
  local copies, waits for them, and re-layouts  42.8 us (6%)
  between operations  13.1 us (2%)
  starting transfers between devices  8.98 us (1%)
  other arithmetic  8.44 us (1%)
    reduce_scatter x3, waiting for transfers between devices, shards(): lax.psum_scatter(make_term(left_block, right_block), 'tok', scatter_dimen...  333 us
    ppermute x3, waiting for transfers between devices, passed_along(): lax.ppermute(value, axis, [(i, (i + by) % size) for i in range(size)])  179 us
    all_to_all x1, blocking collectives, shards(): lax.all_to_all(reduced_tile, 'tok', split_axis=1, concat_axis=0, tiled=True)  86.4 us
    dot_general x3, matrix products, make_term(): lax.dot_general(left_block, right_block, contract_first, preferred_elemen...  43.4 us
    div x2, local copies, waits for them, and re-layouts, shards(): return token_sums / jnp.float32(total_tokens)  17.6 us
    unnamed x15, local copies, waits for them, and re-layouts  17.5 us
  transfers between devices with their start and end apart: 6, of which 5 were waited for; matrix products, arithmetic and copies ran while one was open for 6% of the time, Pallas kernels for 0%

commit v1 on v0

v1 whole, which is shorter than its diff:
```python
import jax
import jax.numpy as jnp
from jax import lax
from jax.experimental import pallas as pl
from jax.experimental.pallas import tpu as pltpu
from jax.sharding import PartitionSpec as P

POWER = 11
SHIFT = 11
SCALE_ROWS = 16
GROUP = 4
LANES = 128
VMEM_BYTES = 60 * 2**20


def encode(sums):
    top = jnp.max(jnp.abs(sums), axis=0, keepdims=True)
    top = jnp.maximum(top, 1e-30).astype(jnp.bfloat16).astype(jnp.float32)
    value = sums * (2.0**SHIFT / top)
    square = value * value
    fourth = square * square
    code = value * square * (fourth * fourth)
    scale = jnp.broadcast_to(top, (SCALE_ROWS, sums.shape[1]))
    return jnp.concatenate([code, scale], axis=0).astype(jnp.bfloat16)


def decode(block):
    wide = block.astype(jnp.float32)
    code, top = wide[:-SCALE_ROWS], wide[-SCALE_ROWS:]
    root = jnp.exp2(jnp.log2(jnp.abs(code)) * (1.0 / POWER))
    return jnp.where(code < 0, -root, root) * (top[:1] * 2.0**-SHIFT)


def dot(left, right):
    return jnp.dot(left, right, preferred_element_type=jnp.float32)


TOKEN = jax.ShapeDtypeStruct((8, LANES), jnp.float32)


class Sequence:
    def __init__(self):
        self.token = []

    def call(self, kernel, outs, operands, **settings):
        results = pl.pallas_call(
            kernel,
            out_shape=[*outs, TOKEN],
            in_specs=[pl.BlockSpec(memory_space=pltpu.HBM)] * (len(operands) + len(self.token)),
            out_specs=[pl.BlockSpec(memory_space=pltpu.HBM)] * (len(outs) + 1),
            cost_estimate=pl.CostEstimate(flops=1024, bytes_accessed=1024, transcendentals=0),
            compiler_params=pltpu.CompilerParams(vmem_limit_bytes=VMEM_BYTES),
            **settings,
        )(*operands, *self.token)
        self.token = [results[-1]]
        return results[:-1]

    def held(self, *values):
        outs = [jax.ShapeDtypeStruct(value.shape, value.dtype) for value in values]
        aliases = {index: index for index in range(len(values))}
        return self.call(lambda *refs: None, outs, values, input_output_aliases=aliases)

    def local(self, body, outs, *operands, into=None):
        count, tokens = len(operands), len(self.token)
        operands = [part if isinstance(part, tuple) else (part, part.shape, None) for part in operands]
        shapes = [out[0] if isinstance(out, tuple) else out for out in outs]
        saved = [out[1] if isinstance(out, tuple) else [out] for out in outs]
        slots = [part for parts in saved for part in parts]
        starts = [sum(map(len, saved[:index])) for index in range(len(saved))]
        numbered = [range(start, start + len(parts)) for start, parts in zip(starts, saved)]
        inputs = count + (into is not None) + tokens

        def kernel(*refs):
            sources, results, scratch = refs[:count], refs[inputs:], refs[inputs + len(outs) + 1 :]
            held_in, held_out, semaphores = scratch[:count], scratch[count:-1], scratch[-1]
            copies = [
                pltpu.make_async_copy(source.at[part[2]()] if part[2] else source, copy, semaphores.at[index])
                for index, (source, part, copy) in enumerate(zip(sources, operands, held_in))
            ]
            for copy in copies:
                copy.start()
            arrived, pending, free = set(), [], [[*numbers] for numbers in numbered]

            def load(index):
                if index not in arrived:
                    copies[index].wait()
                    arrived.add(index)
                return held_in[index]

            def save(index, value, *place):
                slot = free[index].pop(0)
                held_out[slot][...] = value
                target = results[index].at[place] if place else results[index]
                pending.append(pltpu.make_async_copy(held_out[slot], target, semaphores.at[count + slot]))
                pending[-1].start()

            body(load, save)
            for index in range(count):
                load(index)
            for copy in pending:
                copy.wait()

        return self.call(
            kernel,
            shapes,
            [*[part[0] for part in operands], *([] if into is None else [into])],
            scratch_shapes=[
                *[pltpu.VMEM(part[1], part[0].dtype) for part in operands],
                *[pltpu.VMEM(part.shape, part.dtype) for part in slots],
                pltpu.SemaphoreType.DMA((count + len(slots),)),
            ],
            input_output_aliases={} if into is None else {count: 0},
        )


def ring_place(index, cols):
    return index if index < cols // 2 else cols - 1 - (index - cols // 2)


def ring_permute(value, by):
    cols = lax.axis_size("col")
    pairs = [(ring_place(i, cols), ring_place((i + by) % cols, cols)) for i in range(cols)]
    return lax.ppermute(value, "col", pairs)


def narrow_shards(activations):
    block = activations.shape[1]
    toks, cols = lax.axis_size("tok"), lax.axis_size("col")
    col = lax.axis_index("col")
    total_tokens = activations.shape[0] * toks
    half = cols // 2

    def column(offset):
        position = jnp.where(col < half, col, cols - 1 - (col - half))
        position = (position + offset) % cols
        return jnp.where(position < half, position, cols - 1 - (position - half))

    factor_rows = jnp.zeros((block // toks, cols * block), jnp.float32)
    other = activations
    for offset in range(half + 1):
        tile = lax.dot_general(activations, other, (((0,), (0,)), ((), ())), preferred_element_type=jnp.float32)
        rows = lax.psum_scatter(tile, "tok", scatter_dimension=0, tiled=True) / jnp.float32(total_tokens)
        factor_rows = lax.dynamic_update_slice(factor_rows, rows, (0, column(offset) * block))
        if 0 < offset < half:
            turned = lax.all_to_all(rows, "tok", split_axis=1, concat_axis=0, tiled=True).T
            factor_rows = lax.dynamic_update_slice(
                factor_rows, ring_permute(turned, offset), (0, column(-offset) * block)
            )
        if offset < half:
            other = ring_permute(other, -1)
    return factor_rows


def shards(activations):
    tokens, block = activations.shape
    toks = lax.axis_size("tok")
    cols = lax.axis_size("col")
    share = block // toks
    width = 2 * share
    if share % LANES:
        return narrow_shards(activations)
    groups = toks // GROUP
    half = cols // 2
    scale = 1.0 / (tokens * toks)
    steps = range(groups)
    sent_first = [*range(1, groups), 0]

    def along_tok(value, step, other_side=0, other_core=0):
        def target(index):
            return (index + GROUP * step) % toks ^ (2 * other_side + other_core)

        return lax.ppermute(value, "tok", [(i, target(i)) for i in range(toks)])

    def ring_column(offset):
        col = lax.axis_index("col")
        position = jnp.where(col < half, col, cols - 1 - (col - half))
        position = lax.rem(position + offset + cols, cols)
        return jnp.where(position < half, position, cols - 1 - (position - half))

    def feature_start(step, which):
        tok = lax.axis_index("tok")
        group, side = lax.div(tok, GROUP), lax.div(lax.rem(tok, GROUP), 2)
        side = side if which == 0 else 1 - side
        return (lax.rem(group + step, groups) * 2 + side) * width

    def core_start(other_core=0):
        core = lax.rem(lax.axis_index("tok"), 2)
        return (core if other_core == 0 else 1 - core) * share

    names = [(step, which) for which in range(2) for step in sent_first]
    first, second = names[:groups], names[groups:]
    shape = jax.ShapeDtypeStruct
    order = Sequence()
    rows_shape = shape((share, cols * block), jnp.float32)

    def columns(array, start, count):
        return (array, (tokens, count), lambda: (slice(None), pl.ds(pl.multiple_of(start(), LANES), count)))

    def side_features(which, apart):
        def body(load, save):
            for index in range(groups):
                if apart:
                    save(index, load(index)[...])
                else:
                    save(0, load(index)[...], slice(None), pl.ds(index * width, width))

        parts = [columns(activations, lambda step=step: feature_start(step, which), width) for step in sent_first]
        piece = shape((tokens, width), jnp.bfloat16)
        if apart:
            return list(order.local(body, [piece] * groups, *parts))
        return order.local(body, [(shape((tokens, groups * width), jnp.bfloat16), [piece] * groups)], *parts)[0]

    own = [None, side_features(1, False)]
    mate = along_tok(activations, 0, 0, 1)
    near = [along_tok(own[1], 0, 1), [None] * groups]
    near_mate = [None, [None] * groups]
    own[0] = side_features(0, True)

    def at(source, step, start, count):
        index = sent_first.index(step)
        if isinstance(source, list):
            return columns(source[index], start, count)
        return columns(source, lambda: index * width + start(), count)

    def row_part(source, step):
        if source is mate:
            return columns(mate, lambda: feature_start(step, 0) + core_start(), share)
        return at(source, step, core_start, share)

    def row_operand(sources, step):
        count = len(sources)

        def body(load, save):
            save(0, jnp.concatenate([load(index)[...].T for index in range(count)], axis=1))

        out = shape((share, count * tokens), jnp.bfloat16)
        return order.local(body, [out], *[row_part(source, step) for source in sources])[0]

    def operands(rows, blocks):
        arrays, table = [*rows], {}

        for step, which in blocks:
            parts = [at(source[which], step, lambda: 0, width) for source in (own, near, near_mate)]
            parts.insert(1, columns(mate, lambda step=step, which=which: feature_start(step, which), width))
            table[step, which] = range(len(arrays), len(arrays) + 4)
            arrays += parts
        return arrays, table

    def product(load, rows, table, name):
        total = None
        each = 4 // len(rows)
        for number, slot in enumerate(table[name]):
            left = load(number // each)[:, (number % each) * tokens : (number % each + 1) * tokens]
            term = dot(left, load(slot)[...])
            total = term if total is None else total + term
        return total

    def own_sums(rows, blocks):
        arrays, table = operands(rows, blocks)

        def body(load, save):
            for index, name in enumerate(blocks):
                save(0, product(load, rows, table, name), slice(None), pl.ds(index * width, width))

        value_shape = shape((share, width), jnp.float32)
        out = (shape((share, len(blocks) * width), jnp.float32), [value_shape] * len(blocks))
        return order.local(body, [out], *arrays)[0]

    def code_of(blocks):
        return shape((share + SCALE_ROWS, len(blocks) * width), jnp.bfloat16)

    def partial_sums(rows, blocks):
        arrays, table = operands(rows, blocks)

        def body(load, save):
            for index, name in enumerate(blocks):
                code = encode(product(load, rows, table, name))
                save(0, code, slice(None), pl.ds(index * width, width))

        piece = shape((share + SCALE_ROWS, width), jnp.bfloat16)
        return order.local(body, [(code_of(blocks), [piece] * len(blocks))], *arrays)[0]

    def totals(offset, rows, blocks, arrived, into, ready=None):
        arrays, table = operands(rows, blocks) if ready is None else ([ready], None)
        mirrored = 0 < offset < half
        place = {}
        for back, codes in enumerate(arrived, 1):
            for code, code_blocks in codes:
                arrays.append(code)
                for index, (step, which) in enumerate(code_blocks):
                    place[back, ((step - back) % groups, which)] = (len(arrays) - 1, index * width)

        def body(load, save):
            for index, name in enumerate(blocks):
                if ready is None:
                    value = product(load, rows, table, name)
                else:
                    value = load(0)[:, index * width : (index + 1) * width]
                for back in range(1, groups):
                    slot, start = place[back, name]
                    value = value + decode(load(slot)[:, start : start + width])
                if offset == 0:
                    start = ring_column(0) * block + feature_start(*name)
                    save(0, value * scale, slice(None), pl.ds(pl.multiple_of(start, LANES), width))
                else:
                    save(0, encode(value), slice(None), pl.ds(index * width, width))
                    if mirrored:
                        save(1, value, slice(None), pl.ds(index * width, width))

        value_shape = shape((share, width), jnp.float32)
        if offset == 0:
            outs = [(rows_shape, [value_shape] * len(blocks))]
        else:
            outs = [(code_of(blocks), [shape((share + SCALE_ROWS, width), jnp.bfloat16)] * len(blocks))]
        if mirrored:
            outs.append((shape((share, len(blocks) * width), jnp.float32), [value_shape] * len(blocks)))
        return order.local(body, outs, *arrays, into=into)

    def turned_pieces(value):
        def body(load, save):
            for index in range(len(names)):
                turned = load(0)[:, index * width : (index + 1) * width].T
                first_core = jnp.full((1, share), core_start(), jnp.int32) == 0
                one, two = turned[:share], turned[share:]
                same = jnp.where(first_core, one, two)
                other = jnp.where(first_core, two, one)
                save(index, encode(jnp.concatenate([same, other], axis=0)))

        return order.local(body, [shape((width + SCALE_ROWS, share), jnp.bfloat16)] * len(names), value)

    def for_mate(pieces):
        def body(load, save):
            parts = [load(index)[share:] for index in range(len(names))]
            save(0, jnp.concatenate(parts, axis=0))

        return order.local(
            body, [shape((len(names) * (share + SCALE_ROWS), share), jnp.bfloat16)], *pieces
        )[0]

    def place_returned(offset, code, blocks, into):
        def body(load, save):
            for index, name in enumerate(blocks):
                value = decode(load(0)[:, index * width : (index + 1) * width]) * scale
                start = ring_column(offset) * block + feature_start(*name)
                save(0, value, slice(None), pl.ds(pl.multiple_of(start, LANES), width))

        value_shape = shape((share, width), jnp.float32)
        return order.local(body, [(rows_shape, [value_shape] * len(blocks))], code, into=into)[0]

    def place_mirrored(offset, pieces, from_mate, into):
        def body(load, save):
            for index, (step, which) in enumerate(names):
                rows = share + SCALE_ROWS
                piece = load(index)
                mine = jnp.concatenate([piece[:share], piece[width:]], axis=0)
                for other_core, code in enumerate((mine, load(len(names))[index * rows : (index + 1) * rows])):
                    start = feature_start((groups - step) % groups, which) + core_start(other_core)
                    start = ring_column(-offset) * block + start
                    save(0, decode(code) * scale, slice(None), pl.ds(pl.multiple_of(start, LANES), share))

        value_shape = shape((share, share), jnp.float32)
        return order.local(
            body, [(rows_shape, [value_shape] * (2 * len(names)))], *pieces, from_mate, into=into
        )[0]

    left = [{step: [] for step in steps} for offset in range(half + 1)]
    sent_steps = range(1, groups)

    def start_rows(pair, turn):
        backward = {}
        for step in sent_steps:
            rows = row_operand(pair, step)
            left[0][step].append(rows)
            for offset in range(1, half):
                rows = ring_permute(rows, 1)
                left[offset][step].append(rows)
            if turn:
                backward[step] = ring_permute(left[0][step][-1], -1)
        return backward

    def relayed(backward):
        for hop in range(1, half):
            for step in sent_steps:
                backward[step] = ring_permute(order.held(backward[step])[0], -1)
        return backward

    def send(offset, blocks):
        return [(along_tok(partial_sums(left[offset][step], blocks), step), blocks) for step in sent_steps]

    def settled(sent):
        return [(order.held(code)[0], blocks) for code, blocks in sent]

    def settle(offset):
        for step in sent_steps:
            left[offset][step][-1] = order.held(left[offset][step][-1])[0]

    def computed(offset, blocks):
        return [partial_sums(left[offset][step], blocks) for step in sent_steps]

    def sent(codes, blocks):
        return [(along_tok(order.held(code)[0], step), blocks) for step, code in zip(sent_steps, codes)]

    inner = range(1, half)
    sums = {}
    def from_near(index):
        near[1][index] = order.held(near[1][index])[0]
        near_mate[1][index] = along_tok(near[1][index], 0, 0, 1)

    def to_near(index):
        near[1][index] = along_tok(own[0][index], 0, 1)

    backward = start_rows([own[0], mate], True)
    for offset in inner:
        settle(offset)
    backward = relayed(backward)
    near[0], *own[0] = order.held(near[0], *own[0])
    near_mate[0] = along_tok(near[0], 0, 0, 1)
    to_near(0)
    start_rows([near[0], near_mate[0]], False)
    sums[0, 0] = send(0, first)
    here = row_operand([own[0], mate, near[0], near_mate[0]], 0)
    left[0][0] = [here]
    for offset in inner:
        left[offset][0] = [ring_permute(here, offset)]
    opposite = ring_permute(here, -1)
    for step in sent_steps:
        left[half][step].append(order.held(backward[step])[0])
    from_near(0)
    for offset in inner:
        settle(offset)
    for step in sent_steps:
        left[half][step].append(ring_permute(left[half - 1][step][-1], 1))
    for index in range(1, groups):
        own[0][index] = order.held(own[0][index])[0]
        to_near(index)
    codes = {offset: computed(offset, first) for offset in inner}
    sums[0, 0] = settled(sums[0, 0])
    for offset in inner:
        sums[offset, 0] = sent(codes[offset], first)
    factor_rows = totals(0, left[0][0], first, [[part] for part in sums[0, 0]], None)[0]
    for step in sent_steps:
        left[half][step][-1] = order.held(left[half][step][-1])[0]
    codes = computed(half, first)
    for offset in inner:
        sums[offset, 0] = settled(sums[offset, 0])
    for index in range(1, groups):
        from_near(index)
    sums[half, 0] = sent(codes, first)
    for offset in inner:
        sums[offset, 1] = send(offset, second)
    codes = computed(half, second)
    sums[half, 0] = settled(sums[half, 0])
    for hop in range(1, half):
        opposite = ring_permute(order.held(opposite)[0], -1)
    left[half][0] = [opposite]
    last = computed(0, second)
    ready = own_sums(left[0][0], second)
    for offset in inner:
        left[offset][0] = order.held(*left[offset][0])
    for offset in inner:
        sums[offset, 1] = settled(sums[offset, 1])
    sums[half, 1] = sent(codes, second)

    turned, returned, values = {}, {}, {}
    for offset in inner:
        parts = [list(pair) for pair in zip(sums[offset, 0], sums[offset, 1])]
        code, values[offset] = totals(offset, left[offset][0], names, parts, None)
        returned[offset] = ring_permute(code, -offset)
    for offset in inner:
        pieces = turned_pieces(values[offset])
        turned[offset] = [
            piece if name == (0, 0) else along_tok(piece, *name) for name, piece in zip(names, pieces)
        ]
    returned[half] = []
    for which, blocks in enumerate((first, second)):
        if which:
            sums[half, 1] = settled(sums[half, 1])
            for offset in inner:
                inside = names.index((0, 1))
                turned[offset][inside] = order.held(turned[offset][inside])[0]
        code = totals(half, left[half][0], blocks, [[part] for part in sums[half, which]], None)[0]
        returned[half].append(ring_permute(code, -half))
    for offset in inner:
        turned[offset] = order.held(*turned[offset])
    sums[0, 1] = sent(last, second)
    for offset in inner:
        turned[offset] = [*turned[offset], along_tok(for_mate(turned[offset]), 0, 0, 1)]
    for offset in inner:
        factor_rows = place_returned(offset, returned[offset], names, factor_rows)
    for blocks, code in zip((first, second), returned[half]):
        factor_rows = place_returned(half, code, blocks, factor_rows)
    for offset in inner:
        factor_rows = place_mirrored(offset, turned[offset][:-1], turned[offset][-1], factor_rows)
    return totals(0, None, second, [[part] for part in sums[0, 1]], factor_rows, ready)[0]


def solution(mesh):
    in_specs = (P("tok", "col"),)
    out_specs = P(("col", "tok"), None)
    return jax.shard_map(shards, mesh=mesh, in_specs=in_specs, out_specs=out_specs, check_vma=False)
```

time: 716 us -> 278 us (0.39)
  waiting for transfers between devices: 513 us -> 108 us
  Pallas kernels: 0 us -> 113 us
  blocking collectives: 86.4 us -> 0 us
  matrix products: 43.4 us -> 0 us
  starting transfers between devices: 8.98 us -> 36.2 us
  local copies, waits for them, and re-layouts: 42.8 us -> 16 us
  between operations: 13.1 us -> 0.63 us
  other arithmetic: 8.44 us -> 0 us
    reduce_scatter x3 -> x0, waiting for transfers between devices: 333 us -> none  [shards(): lax.psum_scatter(make_term(left_block, right_block), 'tok', scatter_dimen...]
    pallas_call x0 -> x45, Pallas kernels: none -> 113 us  [call(): pl.pallas_call(kernel, out_shape=[*outs, TOKEN], in_specs=[pl.BlockSpec(m...]
    all_to_all x1 -> x0, blocking collectives: 86.4 us -> none  [shards(): lax.all_to_all(reduced_tile, 'tok', split_axis=1, concat_axis=0, tiled=True)]
    ppermute x3 -> x28, waiting for transfers between devices: 179 us -> 108 us  [the longest x17 65.1 us: along_tok(): return lax.ppermute(value, 'tok', [(i, target(i)) for i in range(toks)])]
    dot_general x3 -> x0, matrix products: 43.4 us -> none  [make_term(): lax.dot_general(left_block, right_block, contract_first, preferred_elemen...]
    ppermute x3 -> x28, starting transfers between devices: 8.89 us -> 36.2 us  [the longest x17 19.8 us: along_tok(): return lax.ppermute(value, 'tok', [(i, target(i)) for i in range(toks)])]
    div x2 -> x0, local copies, waits for them, and re-layouts: 17.6 us -> none  [shards(): return token_sums / jnp.float32(total_tokens)]
    div x1 -> x0, other arithmetic: 8.44 us -> none  [shards(): return token_sums / jnp.float32(total_tokens)]
  transfers between devices with their start and end apart: 6 -> 28, of which waited for: 5 -> 15; matrix products, arithmetic and copies ran while one was open for 6% -> 0% of each run, Pallas kernels for 0% -> 40%
where the time goes in v1:
time: 278 us; the launch traced here: 273 us
  Pallas kernels  113 us (41%)
  waiting for transfers between devices  108 us (39%)
  starting transfers between devices  36.2 us (13%)
  local copies, waits for them, and re-layouts  16 us (6%)
    pallas_call x45, Pallas kernels, call(): pl.pallas_call(kernel, out_shape=[*outs, TOKEN], in_specs=[pl.BlockSpec(m...  113 us
    ppermute x17, waiting for transfers between devices, along_tok(): return lax.ppermute(value, 'tok', [(i, target(i)) for i in range(toks)])  65.1 us
    ppermute x11, waiting for transfers between devices, ring_permute(): return lax.ppermute(value, 'col', pairs)  42.5 us
    ppermute x17, starting transfers between devices, along_tok(): return lax.ppermute(value, 'tok', [(i, target(i)) for i in range(toks)])  19.8 us
    ppermute x11, starting transfers between devices, ring_permute(): return lax.ppermute(value, 'col', pairs)  16.3 us
    unnamed x44, local copies, waits for them, and re-layouts  16 us
  transfers between devices with their start and end apart: 28, of which 15 were waited for; matrix products, arithmetic and copies ran while one was open for 0% of the time, Pallas kernels for 40%

profile of v1, /device:TPU:0, one launch (start us, length us, event | category | flops | bytes accessed | tf_op | source)
XLA Modules:
  0.0 273.1 jit_solution(15541526234988205639)
XLA Ops:
  13.1 23.5 %collective-permute-done.3.refs_0_ = bf16[256,2048]{1,0:T(8,128)(2,1)S(1)} collective-permute-done((bf16[256,2048]{1,0:T(8,128)(2,1)}, bf16[256,2048]{1,0:T(8,128)(2,1)S(1)}, u32[]{:S(2)}, u32[]{:S(2)}) %collective-permute-start.3) | collective-permute-done | bytes 1048608 | tf_op jit(solution)/shard_map/ppermute | solution.py:123
  38.2 14.1 %collective-permute-done.refs_0_ = bf16[1024,1024]{1,0:T(8,128)(2,1)S(1)} collective-permute-done((bf16[1024,1024]{1,0:T(8,128)(2,1)}, bf16[1024,1024]{1,0:T(8,128)(2,1)S(1)}, u32[]{:S(2)}, u32[]{:S(2)}) %collective-permute-start) | collective-permute-done | bytes 2097184 | tf_op jit(solution)/shard_map/ppermute | solution.py:172
  63.5 6.5 %shard_map.24 = (bf16[272,1024]{1,0:T(8,128)(2,1)}, f32[8,128]{1,0:T(8,128)}) custom-call(bf16[256,2048]{1,0:T(8,128)(2,1)} %get-tuple-element.109.refs_0_, bf16[256,2048]{1,0:T(8,128)(2,1)} %get-tuple-element.116.refs_1_, bf16[1024,512]{1,0:T(8,128)(2,1)} %get-tuple-element.117.refs_2_.refs_1_, ...), custom_call_target="tpu_custom_call" | custom-call | flops 1024 | bytes 1024 | tf_op jit(solution)/shard_map/pallas_call | solution.py:46
  76.0 3.5 %collective-permute-done.6.refs_0_ = bf16[256,2048]{1,0:T(8,128)(2,1)} collective-permute-done((bf16[256,2048]{1,0:T(8,128)(2,1)}, bf16[256,2048]{1,0:T(8,128)(2,1)}, u32[]{:S(2)}, u32[]{:S(2)}) %collective-permute-start.6) | collective-permute-done | bytes 1048608 | tf_op jit(solution)/shard_map/ppermute | solution.py:123
  79.5 10.6 %collective-permute-done.5.refs_0_ = bf16[1024,512]{1,0:T(8,128)(2,1)S(1)} collective-permute-done((bf16[1024,512]{1,0:T(8,128)(2,1)}, bf16[1024,512]{1,0:T(8,128)(2,1)S(1)}, u32[]{:S(2)}, u32[]{:S(2)}) %collective-permute-start.5) | collective-permute-done | bytes 1048608 | tf_op jit(solution)/shard_map/ppermute | solution.py:172
  95.1 6.6 %shard_map.30 = (bf16[272,1024]{1,0:T(8,128)(2,1)}, f32[8,128]{1,0:T(8,128)}) custom-call(bf16[256,2048]{1,0:T(8,128)(2,1)} %get-tuple-element.128.refs_0_, bf16[256,2048]{1,0:T(8,128)(2,1)} %get-tuple-element.129.refs_1_, bf16[1024,512]{1,0:T(8,128)(2,1)} %get-tuple-element.117.refs_2_.refs_1_, ...), custom_call_target="tpu_custom_call" | custom-call | flops 1024 | bytes 1024 | tf_op jit(solution)/shard_map/pallas_call | solution.py:46
  104.4 6.9 %shard_map.33 = (f32[256,8192]{1,0:T(8,128)}, f32[8,128]{1,0:T(8,128)}) custom-call(bf16[256,4096]{1,0:T(8,128)(2,1)} %get-tuple-element.120.refs_0_, bf16[1024,512]{1,0:T(8,128)(2,1)} %get-tuple-element.117.refs_2_.refs_1_, bf16[1024,2048]{1,0:T(8,128)(2,1)} %collective-permute-done.1.refs_1_.refs_3_.refs_7_.refs_2_.refs_6_.refs_10_.refs_14_, ...), custom_call_target="tpu_custom_call" | custom-call | flops 1024 | bytes 1024 | tf_op jit(solution)/shard_map/pallas_call | solution.py:46
  111.3 6.2 %collective-permute-done.12.refs_0_ = bf16[256,2048]{1,0:T(8,128)(2,1)} collective-permute-done((bf16[256,2048]{1,0:T(8,128)(2,1)}, bf16[256,2048]{1,0:T(8,128)(2,1)}, u32[]{:S(2)}, u32[]{:S(2)}) %collective-permute-start.12) | collective-permute-done | bytes 1048608 | tf_op jit(solution)/shard_map/ppermute | solution.py:123
  117.6 6.5 %shard_map.35 = (bf16[272,1024]{1,0:T(8,128)(2,1)}, f32[8,128]{1,0:T(8,128)}) custom-call(bf16[256,2048]{1,0:T(8,128)(2,1)} %get-tuple-element.136.refs_0_, bf16[256,2048]{1,0:T(8,128)(2,1)} %get-tuple-element.140.refs_1_, bf16[1024,512]{1,0:T(8,128)(2,1)} %get-tuple-element.117.refs_2_.refs_1_, ...), custom_call_target="tpu_custom_call" | custom-call | flops 1024 | bytes 1024 | tf_op jit(solution)/shard_map/pallas_call | solution.py:46
  124.1 5.3 %collective-permute-done.11.refs_0_ = bf16[272,1024]{1,0:T(8,128)(2,1)S(1)} collective-permute-done((bf16[272,1024]{1,0:T(8,128)(2,1)}, bf16[272,1024]{1,0:T(8,128)(2,1)S(1)}, u32[]{:S(2)}, u32[]{:S(2)}) %collective-permute-start.11) | collective-permute-done | bytes 557088 | tf_op jit(solution)/shard_map/ppermute | solution.py:172
  137.8 6.5 %shard_map.39 = (bf16[272,1024]{1,0:T(8,128)(2,1)}, f32[8,128]{1,0:T(8,128)}) custom-call(bf16[256,2048]{1,0:T(8,128)(2,1)} %get-tuple-element.128.refs_0_, bf16[256,2048]{1,0:T(8,128)(2,1)} %get-tuple-element.129.refs_1_, bf16[1024,1024]{1,0:T(8,128)(2,1)} %get-tuple-element.104.refs_2_.refs_6_.refs_1_.refs_5_.refs_9_.refs_13_, ...), custom_call_target="tpu_custom_call" | custom-call | flops 1024 | bytes 1024 | tf_op jit(solution)/shard_map/pallas_call | solution.py:46
  144.3 6.5 %shard_map.40 = (bf16[272,1024]{1,0:T(8,128)(2,1)}, f32[8,128]{1,0:T(8,128)}) custom-call(bf16[256,2048]{1,0:T(8,128)(2,1)} %get-tuple-element.136.refs_0_, bf16[256,2048]{1,0:T(8,128)(2,1)} %get-tuple-element.140.refs_1_, bf16[1024,1024]{1,0:T(8,128)(2,1)} %get-tuple-element.104.refs_2_.refs_6_.refs_1_.refs_5_.refs_9_.refs_13_, ...), custom_call_target="tpu_custom_call" | custom-call | flops 1024 | bytes 1024 | tf_op jit(solution)/shard_map/pallas_call | solution.py:46
  150.8 9.6 %collective-permute-done.15.refs_0_ = bf16[272,1024]{1,0:T(8,128)(2,1)S(1)} collective-permute-done((bf16[272,1024]{1,0:T(8,128)(2,1)}, bf16[272,1024]{1,0:T(8,128)(2,1)S(1)}, u32[]{:S(2)}, u32[]{:S(2)}) %collective-permute-start.15) | collective-permute-done | bytes 557088 | tf_op jit(solution)/shard_map/ppermute | solution.py:172
  162.6 6.5 %shard_map.43 = (bf16[272,1024]{1,0:T(8,128)(2,1)}, f32[8,128]{1,0:T(8,128)}) custom-call(bf16[256,2048]{1,0:T(8,128)(2,1)} %get-tuple-element.109.refs_0_, bf16[256,2048]{1,0:T(8,128)(2,1)} %get-tuple-element.116.refs_1_, bf16[1024,1024]{1,0:T(8,128)(2,1)} %get-tuple-element.104.refs_2_.refs_6_.refs_1_.refs_5_.refs_9_.refs_13_, ...), custom_call_target="tpu_custom_call" | custom-call | flops 1024 | bytes 1024 | tf_op jit(solution)/shard_map/pallas_call | solution.py:46
  169.1 6.1 %shard_map.44 = (f32[256,1024]{1,0:T(8,128)}, f32[8,128]{1,0:T(8,128)}) custom-call(bf16[256,4096]{1,0:T(8,128)(2,1)} %get-tuple-element.120.refs_0_, bf16[1024,1024]{1,0:T(8,128)(2,1)} %get-tuple-element.104.refs_2_.refs_6_.refs_1_.refs_5_.refs_9_.refs_13_, ...), custom_call_target="tpu_custom_call" | custom-call | flops 1024 | bytes 1024 | tf_op jit(solution)/shard_map/pallas_call | solution.py:46
  175.2 7.2 %collective-permute-done.16.refs_0_ = bf16[256,4096]{1,0:T(8,128)(2,1)} collective-permute-done((bf16[256,4096]{1,0:T(8,128)(2,1)}, bf16[256,4096]{1,0:T(8,128)(2,1)}, u32[]{:S(2)}, u32[]{:S(2)}) %collective-permute-start.16) | collective-permute-done | bytes 2097184 | tf_op jit(solution)/shard_map/ppermute | solution.py:123
  182.4 7.2 %collective-permute-done.17.refs_0_ = bf16[272,1024]{1,0:T(8,128)(2,1)S(1)} collective-permute-done((bf16[272,1024]{1,0:T(8,128)(2,1)}, bf16[272,1024]{1,0:T(8,128)(2,1)S(1)}, u32[]{:S(2)}, u32[]{:S(2)}) %collective-permute-start.17) | collective-permute-done | bytes 557088 | tf_op jit(solution)/shard_map/ppermute | solution.py:172
  190.4 13.9 %shard_map.48 = (bf16[272,2048]{1,0:T(8,128)(2,1)}, f32[256,2048]{1,0:T(8,128)}, f32[8,128]{1,0:T(8,128)}) custom-call(bf16[256,4096]{1,0:T(8,128)(2,1)} %get-tuple-element.157.refs_0_, bf16[1024,512]{1,0:T(8,128)(2,1)} %get-tuple-element.117.refs_2_.refs_1_, ...), custom_call_target="tpu_custom_call" | custom-call | flops 1024 | bytes 1024 | tf_op jit(solution)/shard_map/pallas_call | solution.py:46
  206.2 3.6 %shard_map.49 = (bf16[528,256]{1,0:T(8,128)(2,1)}, bf16[528,256]{1,0:T(8,128)(2,1)}, bf16[528,256]{1,0:T(8,128)(2,1)}, bf16[528,256]{1,0:T(8,128)(2,1)}, f32[8,128]{1,0:T(8,128)}) custom-call(f32[256,2048]{1,0:T(8,128)} %get-tuple-element.165.refs_0_, f32[8,128]{1,0:T(8,128)} %get-tuple-element.166.refs_1_), custom_call_target="tpu_custom_call" | custom-call | flops 1024 | bytes 1024 | tf_op jit(solution)/shard_map/pallas_call | solution.py:46
  214.3 7.3 %shard_map.50 = (bf16[272,1024]{1,0:T(8,128)(2,1)}, f32[8,128]{1,0:T(8,128)}) custom-call(bf16[256,4096]{1,0:T(8,128)(2,1)} %copy-done.9, bf16[1024,512]{1,0:T(8,128)(2,1)} %get-tuple-element.117.refs_2_.refs_1_, bf16[1024,2048]{1,0:T(8,128)(2,1)} %collective-permute-done.1.refs_1_.refs_3_.refs_7_.refs_2_.refs_6_.refs_10_.refs_14_, ...), custom_call_target="tpu_custom_call" | custom-call | flops 1024 | bytes 1024 | tf_op jit(solution)/shard_map/pallas_call | solution.py:46
  222.8 4.8 %collective-permute-done.20.refs_0_ = bf16[528,256]{1,0:T(8,128)(2,1)S(1)} collective-permute-done((bf16[528,256]{1,0:T(8,128)(2,1)}, bf16[528,256]{1,0:T(8,128)(2,1)S(1)}, u32[]{:S(2)}, u32[]{:S(2)}) %collective-permute-start.20) | collective-permute-done | bytes 270368 | tf_op jit(solution)/shard_map/ppermute | solution.py:172
  228.3 7.3 %shard_map.53 = (bf16[272,1024]{1,0:T(8,128)(2,1)}, f32[8,128]{1,0:T(8,128)}) custom-call(bf16[256,4096]{1,0:T(8,128)(2,1)} %copy-done.9, bf16[1024,1024]{1,0:T(8,128)(2,1)} %get-tuple-element.104.refs_2_.refs_6_.refs_1_.refs_5_.refs_9_.refs_13_, bf16[1024,2048]{1,0:T(8,128)(2,1)} %collective-permute-done.1.refs_1_.refs_3_.refs_7_.refs_2_.refs_6_.refs_10_.refs_14_, ...), custom_call_target="tpu_custom_call" | custom-call | flops 1024 | bytes 1024 | tf_op jit(solution)/shard_map/pallas_call | solution.py:46
  239.8 4.2 %collective-permute-start.23 = (bf16[272,1024]{1,0:T(8,128)(2,1)}, bf16[272,1024]{1,0:T(8,128)(2,1)S(1)}, u32[]{:S(2)}, u32[]{:S(2)}) collective-permute-start(bf16[272,1024]{1,0:T(8,128)(2,1)} %get-tuple-element.182), channel_id=1, source_target_pairs={{0,4},{1,5},{2,6},{3,7},{4,0},{5,1},{6,2},{7,3},{8,12},{9,13},{10,... | collective-permute-start | bytes 1671176 | tf_op jit(solution)/shard_map/ppermute | solution.py:172
  258.1 11.2 %collective-permute-done.23.refs_1_ = bf16[272,1024]{1,0:T(8,128)(2,1)S(1)} collective-permute-done((bf16[272,1024]{1,0:T(8,128)(2,1)}, bf16[272,1024]{1,0:T(8,128)(2,1)S(1)}, u32[]{:S(2)}, u32[]{:S(2)}) %collective-permute-start.23) | collective-permute-done | bytes 557088 | tf_op jit(solution)/shard_map/ppermute | solution.py:172
  (121 shorter events, 80.6 us)
Async XLA Ops:
  3.2 49.2 %collective-permute-start = (bf16[1024,1024]{1,0:T(8,128)(2,1)}, bf16[1024,1024]{1,0:T(8,128)(2,1)S(1)}, u32[]{:S(2)}, u32[]{:S(2)}) collective-permute-start(bf16[1024,1024]{1,0:T(8,128)(2,1)} %get-tuple-element.104.refs_2_.refs_6_.refs_1_.refs_5_.refs_9_.refs_13_), channel_id=1, source_target_pairs={{0,2},{1,3},{2,0},{3,1},{4,6},{5,7},{6,4},{7,5},{8,10},{9,11},{10,... | collective-permute-start | bytes 6291464 | tf_op jit(solution)/shard_map/ppermute | solution.py:172
  11.0 25.6 %collective-permute-start.3 = (bf16[256,2048]{1,0:T(8,128)(2,1)}, bf16[256,2048]{1,0:T(8,128)(2,1)S(1)}, u32[]{:S(2)}, u32[]{:S(2)}) collective-permute-start(bf16[256,2048]{1,0:T(8,128)(2,1)} %get-tuple-element.109.refs_0_), channel_id=1, source_target_pairs={{0,8},{8,24},{24,16},{16,0},{1,9},{9,25},{25,17},{17,1},{2,10},{10... | collective-permute-start | bytes 3145736 | tf_op jit(solution)/shard_map/ppermute | solution.py:123
  13.0 25.2 %collective-permute-start.2 = (bf16[256,2048]{1,0:T(8,128)(2,1)}, bf16[256,2048]{1,0:T(8,128)(2,1)}, u32[]{:S(2)}, u32[]{:S(2)}) collective-permute-start(bf16[256,2048]{1,0:T(8,128)(2,1)} %get-tuple-element.109.refs_0_), channel_id=1, source_target_pairs={{0,16},{8,0},{24,8},{16,24},{1,17},{9,1},{25,9},{17,25},{2,18},{10... | collective-permute-start | bytes 3145736 | tf_op jit(solution)/shard_map/ppermute | solution.py:123
  53.6 25.9 %collective-permute-start.6 = (bf16[256,2048]{1,0:T(8,128)(2,1)}, bf16[256,2048]{1,0:T(8,128)(2,1)}, u32[]{:S(2)}, u32[]{:S(2)}) collective-permute-start(bf16[256,2048]{1,0:T(8,128)(2,1)} %get-tuple-element.121), channel_id=1, source_target_pairs={{0,16},{8,0},{24,8},{16,24},{1,17},{9,1},{25,9},{17,25},{2,18},{10... | collective-permute-start | bytes 3145736 | tf_op jit(solution)/shard_map/ppermute | solution.py:123
  55.3 34.8 %collective-permute-start.5 = (bf16[1024,512]{1,0:T(8,128)(2,1)}, bf16[1024,512]{1,0:T(8,128)(2,1)S(1)}, u32[]{:S(2)}, u32[]{:S(2)}) collective-permute-start(bf16[1024,512]{1,0:T(8,128)(2,1)} %get-tuple-element.117.refs_2_.refs_1_), channel_id=1, source_target_pairs={{0,2},{1,3},{2,0},{3,1},{4,6},{5,7},{6,4},{7,5},{8,10},{9,11},{10,... | collective-permute-start | bytes 3145736 | tf_op jit(solution)/shard_map/ppermute | solution.py:172
  61.8 29.3 %collective-permute-start.8 = (bf16[256,2048]{1,0:T(8,128)(2,1)}, bf16[256,2048]{1,0:T(8,128)(2,1)S(1)}, u32[]{:S(2)}, u32[]{:S(2)}) collective-permute-start(bf16[256,2048]{1,0:T(8,128)(2,1)} %get-tuple-element.116.refs_1_), channel_id=1, source_target_pairs={{0,8},{8,24},{24,16},{16,0},{1,9},{9,25},{25,17},{17,1},{2,10},{10... | collective-permute-start | bytes 3145736 | tf_op jit(solution)/shard_map/ppermute | solution.py:123
  70.0 31.7 %collective-permute-start.10 = (bf16[272,1024]{1,0:T(8,128)(2,1)}, bf16[272,1024]{1,0:T(8,128)(2,1)S(1)}, u32[]{:S(2)}, u32[]{:S(2)}) collective-permute-start(bf16[272,1024]{1,0:T(8,128)(2,1)} %get-tuple-element.132), channel_id=1, source_target_pairs={{0,4},{1,5},{2,6},{3,7},{4,0},{5,1},{6,2},{7,3},{8,12},{9,13},{10,... | collective-permute-start | bytes 1671176 | tf_op jit(solution)/shard_map/ppermute | solution.py:172
  92.1 25.5 %collective-permute-start.12 = (bf16[256,2048]{1,0:T(8,128)(2,1)}, bf16[256,2048]{1,0:T(8,128)(2,1)}, u32[]{:S(2)}, u32[]{:S(2)}) collective-permute-start(bf16[256,2048]{1,0:T(8,128)(2,1)} %get-tuple-element.129.refs_1_), channel_id=1, source_target_pairs={{0,8},{8,24},{24,16},{16,0},{1,9},{9,25},{25,17},{17,1},{2,10},{10... | collective-permute-start | bytes 3145736 | tf_op jit(solution)/shard_map/ppermute | solution.py:123
  92.1 39.3 %collective-permute-start.9 = (bf16[1024,512]{1,0:T(8,128)(2,1)}, bf16[1024,512]{1,0:T(8,128)(2,1)S(1)}, u32[]{:S(2)}, u32[]{:S(2)}) collective-permute-start(bf16[1024,512]{1,0:T(8,128)(2,1)} %get-tuple-element.127.refs_6_.refs_5_), channel_id=1, source_target_pairs={{0,2},{1,3},{2,0},{3,1},{4,6},{5,7},{6,4},{7,5},{8,10},{9,11},{10,... | collective-permute-start | bytes 3145736 | tf_op jit(solution)/shard_map/ppermute | solution.py:172
  92.1 69.2 %collective-permute-start.14 = (bf16[256,4096]{1,0:T(8,128)(2,1)}, bf16[256,4096]{1,0:T(8,128)(2,1)}, u32[]{:S(2)}, u32[]{:S(2)}) collective-permute-start(bf16[256,4096]{1,0:T(8,128)(2,1)} %get-tuple-element.120.refs_0_), channel_id=1, source_target_pairs={{0,16},{8,0},{24,8},{16,24},{1,17},{9,1},{25,9},{17,25},{2,18},{10... | collective-permute-start | bytes 6291464 | tf_op jit(solution)/shard_map/ppermute | solution.py:123
  102.6 26.9 %collective-permute-start.11 = (bf16[272,1024]{1,0:T(8,128)(2,1)}, bf16[272,1024]{1,0:T(8,128)(2,1)S(1)}, u32[]{:S(2)}, u32[]{:S(2)}) collective-permute-start(bf16[272,1024]{1,0:T(8,128)(2,1)} %get-tuple-element.135), channel_id=1, source_target_pairs={{0,4},{1,5},{2,6},{3,7},{4,0},{5,1},{6,2},{7,3},{8,12},{9,13},{10,... | collective-permute-start | bytes 1671176 | tf_op jit(solution)/shard_map/ppermute | solution.py:172
  104.4 32.0 %collective-permute-start.7 = (bf16[1024,512]{1,0:T(8,128)(2,1)S(1)}, bf16[1024,512]{1,0:T(8,128)(2,1)S(1)}, u32[]{:S(2)}, u32[]{:S(2)}) collective-permute-start(bf16[1024,512]{1,0:T(8,128)(2,1)S(1)} %copy-done.4), channel_id=1, source_target_pairs={{0,1},{1,0},{2,3},{3,2},{4,5},{5,4},{6,7},{7,6},{8,9},{9,8},{10,11... | collective-permute-start | bytes 3145736 | tf_op jit(solution)/shard_map/ppermute | solution.py:172
  132.3 28.1 %collective-permute-start.15 = (bf16[272,1024]{1,0:T(8,128)(2,1)}, bf16[272,1024]{1,0:T(8,128)(2,1)S(1)}, u32[]{:S(2)}, u32[]{:S(2)}) collective-permute-start(bf16[272,1024]{1,0:T(8,128)(2,1)} %get-tuple-element.147), channel_id=1, source_target_pairs={{0,4},{1,5},{2,6},{3,7},{4,0},{5,1},{6,2},{7,3},{8,12},{9,13},{10,... | collective-permute-start | bytes 1671176 | tf_op jit(solution)/shard_map/ppermute | solution.py:172
  134.2 48.2 %collective-permute-start.16 = (bf16[256,4096]{1,0:T(8,128)(2,1)}, bf16[256,4096]{1,0:T(8,128)(2,1)}, u32[]{:S(2)}, u32[]{:S(2)}) collective-permute-start(bf16[256,4096]{1,0:T(8,128)(2,1)} %get-tuple-element.120.refs_0_), channel_id=1, source_target_pairs={{0,8},{8,24},{24,16},{16,0},{1,9},{9,25},{25,17},{17,1},{2,10},{10... | collective-permute-start | bytes 6291464 | tf_op jit(solution)/shard_map/ppermute | solution.py:123
  161.3 51.5 %collective-permute-start.22 = (bf16[256,4096]{1,0:T(8,128)(2,1)}, bf16[256,4096]{1,0:T(8,128)(2,1)S(1)}, u32[]{:S(2)}, u32[]{:S(2)}) collective-permute-start(bf16[256,4096]{1,0:T(8,128)(2,1)} %get-tuple-element.172), channel_id=1, source_target_pairs={{0,16},{8,0},{24,8},{16,24},{1,17},{9,1},{25,9},{17,25},{2,18},{10... | collective-permute-start | bytes 6291464 | tf_op jit(solution)/shard_map/ppermute | solution.py:123
  162.6 27.0 %collective-permute-start.17 = (bf16[272,1024]{1,0:T(8,128)(2,1)}, bf16[272,1024]{1,0:T(8,128)(2,1)S(1)}, u32[]{:S(2)}, u32[]{:S(2)}) collective-permute-start(bf16[272,1024]{1,0:T(8,128)(2,1)} %get-tuple-element.159), channel_id=1, source_target_pairs={{0,4},{1,5},{2,6},{3,7},{4,0},{5,1},{6,2},{7,3},{8,12},{9,13},{10,... | collective-permute-start | bytes 1671176 | tf_op jit(solution)/shard_map/ppermute | solution.py:172
  190.4 31.1 %collective-permute-start.21 = (bf16[272,1024]{1,0:T(8,128)(2,1)}, bf16[272,1024]{1,0:T(8,128)(2,1)S(1)}, u32[]{:S(2)}, u32[]{:S(2)}) collective-permute-start(bf16[272,1024]{1,0:T(8,128)(2,1)} %get-tuple-element.171), channel_id=1, source_target_pairs={{0,4},{1,5},{2,6},{3,7},{4,0},{5,1},{6,2},{7,3},{8,12},{9,13},{10,... | collective-permute-start | bytes 1671176 | tf_op jit(solution)/shard_map/ppermute | solution.py:172
  204.3 39.7 %collective-permute-start.27 = (bf16[272,2048]{1,0:T(8,128)(2,1)}, bf16[272,2048]{1,0:T(8,128)(2,1)}, u32[]{:S(2)}, u32[]{:S(2)}) collective-permute-start(bf16[272,2048]{1,0:T(8,128)(2,1)} %get-tuple-element.191), channel_id=1, source_target_pairs={{0,16},{8,0},{24,8},{16,24},{1,17},{9,1},{25,9},{17,25},{2,18},{10... | collective-permute-start | bytes 3342344 | tf_op jit(solution)/shard_map/ppermute | solution.py:123
  209.8 17.9 %collective-permute-start.20 = (bf16[528,256]{1,0:T(8,128)(2,1)}, bf16[528,256]{1,0:T(8,128)(2,1)S(1)}, u32[]{:S(2)}, u32[]{:S(2)}) collective-permute-start(bf16[528,256]{1,0:T(8,128)(2,1)} %get-tuple-element.170), channel_id=1, source_target_pairs={{0,2},{1,3},{2,0},{3,1},{4,6},{5,7},{6,4},{7,5},{8,10},{9,11},{10,... | collective-permute-start | bytes 811016 | tf_op jit(solution)/shard_map/ppermute | solution.py:172
  211.6 25.2 %collective-permute-start.18 = (bf16[528,256]{1,0:T(8,128)(2,1)}, bf16[528,256]{1,0:T(8,128)(2,1)S(1)}, u32[]{:S(2)}, u32[]{:S(2)}) collective-permute-start(bf16[528,256]{1,0:T(8,128)(2,1)} %get-tuple-element.167), channel_id=1, source_target_pairs={{0,4},{1,5},{2,6},{3,7},{4,0},{5,1},{6,2},{7,3},{8,12},{9,13},{10,... | collective-permute-start | bytes 811016 | tf_op jit(solution)/shard_map/ppermute | solution.py:172
  212.8 24.0 %collective-permute-start.19 = (bf16[528,256]{1,0:T(8,128)(2,1)}, bf16[528,256]{1,0:T(8,128)(2,1)S(1)}, u32[]{:S(2)}, u32[]{:S(2)}) collective-permute-start(bf16[528,256]{1,0:T(8,128)(2,1)} %get-tuple-element.169), channel_id=1, source_target_pairs={{0,6},{1,7},{2,4},{3,5},{4,2},{5,3},{6,0},{7,1},{8,14},{9,15},{10,... | collective-permute-start | bytes 811016 | tf_op jit(solution)/shard_map/ppermute | solution.py:172
  221.6 25.2 %collective-permute-start.26 = (bf16[272,1024]{1,0:T(8,128)(2,1)}, bf16[272,1024]{1,0:T(8,128)(2,1)S(1)}, u32[]{:S(2)}, u32[]{:S(2)}) collective-permute-start(bf16[272,1024]{1,0:T(8,128)(2,1)} %get-tuple-element.190), channel_id=1, source_target_pairs={{0,24},{8,16},{24,0},{16,8},{1,25},{9,17},{25,1},{17,9},{2,26},{10... | collective-permute-start | bytes 1671176 | tf_op jit(solution)/shard_map/ppermute | solution.py:123
  235.6 15.7 %collective-permute-start.25 = (bf16[272,1024]{1,0:T(8,128)(2,1)}, bf16[272,1024]{1,0:T(8,128)(2,1)S(1)}, u32[]{:S(2)}, u32[]{:S(2)}) collective-permute-start(bf16[272,1024]{1,0:T(8,128)(2,1)} %get-tuple-element.189), channel_id=1, source_target_pairs={{0,24},{8,16},{24,0},{16,8},{1,25},{9,17},{25,1},{17,9},{2,26},{10... | collective-permute-start | bytes 1671176 | tf_op jit(solution)/shard_map/ppermute | solution.py:123
  239.8 29.6 %collective-permute-start.23 = (bf16[272,1024]{1,0:T(8,128)(2,1)}, bf16[272,1024]{1,0:T(8,128)(2,1)S(1)}, u32[]{:S(2)}, u32[]{:S(2)}) collective-permute-start(bf16[272,1024]{1,0:T(8,128)(2,1)} %get-tuple-element.182), channel_id=1, source_target_pairs={{0,4},{1,5},{2,6},{3,7},{4,0},{5,1},{6,2},{7,3},{8,12},{9,13},{10,... | collective-permute-start | bytes 1671176 | tf_op jit(solution)/shard_map/ppermute | solution.py:172
  (26 other events, 61.4 us)
